TPU v7x, 128 devices: a whole 4x4x4 slice. The times are simulated.
128 devices in a mesh: leaf: 32 (over x_lo, y, z), blk: 4 (over x_hi, core).
Axes of the slice: x: 4 (x_hi: 2, x_lo: 2; x = x_hi * 2 + x_lo), y: 4, z: 4, core: 2. Of those that a mesh axis runs over, the one named last changes fastest.
Arguments:
- stiffness: bfloat16 [64, 2048, 2048], P('leaf', 'blk'), may hold values from -6 to 6
- modes: bfloat16 [64, 2048, 512], P('leaf', 'blk'), may hold values from -0.125 to 0.125
- basis: bfloat16 [16384, 2048], P('leaf', 'blk'), may hold values from -0.125 to 0.125
- eigen: float32 [64, 512], P('leaf'), may hold values from 20 to 200
- counts: int32 [64], P('leaf'), may hold values from 80 to 400
- ancestry: int32 [64], P('leaf'), may hold values from 0 to 7
Outputs:
- projection: bfloat16 [64, 512, 2048], P('leaf', None, 'blk')
- correction: float32 [16384, 2048], P('leaf', 'blk')
All inputs are finite; a program needn't handle non-finite values.
Results may differ from a plain program's by a relative error of at most 0.018.
Values may be sent and summed in bfloat16 or wider, within the bound.
No kernel may reach another device: no remote copies, remote signals or barrier semaphores. Data moves between devices by JAX's collectives and lax.ppermute only.
A program may use at most 192 MiB of HBM per device.

v0:
```python
import jax
import jax.numpy as jnp
from jax import lax
from jax.sharding import PartitionSpec as P

Q = 2048


def per_device(stiffness, modes, basis, eigen, counts, ancestry):
    sub_dev = stiffness.shape[0]
    col_dev = basis.shape[1]
    partial_value = jnp.einsum("srm,srq->smq", modes, stiffness, preferred_element_type=jnp.float32)
    summed = lax.psum(partial_value, "blk")
    slots = jnp.arange(summed.shape[1], dtype=jnp.int32)
    live = slots[None, :] < counts[:, None]
    coupled = jnp.where(live[:, :, None], summed, 0.0).astype(jnp.bfloat16)
    every = lax.all_gather(basis, "leaf", axis=0, tiled=True)
    blocks = every.reshape(-1, Q, col_dev)
    picked = blocks[ancestry]
    projection = jnp.einsum(
        "smq,sqw->smw", coupled, picked, preferred_element_type=jnp.float32
    ).astype(jnp.bfloat16)
    scaled = (coupled.astype(jnp.float32) / eigen[:, :, None]).astype(jnp.bfloat16)
    terms = jnp.einsum("smq,smw->sqw", scaled, projection, preferred_element_type=jnp.float32)
    count = lax.axis_size("leaf") * basis.shape[0]
    rows_here = jnp.arange(count, dtype=jnp.int32)
    owner = rows_here // Q
    within = rows_here % Q
    total = jnp.zeros((count, col_dev), jnp.float32)
    for index in range(sub_dev):
        taken = jnp.take(terms[index], within, axis=0)
        match = (owner == ancestry[index])[:, None]
        total = total + jnp.where(match, taken, 0.0)
    correction = lax.psum_scatter(
        total.astype(jnp.bfloat16), "leaf", scatter_dimension=0, tiled=True
    ).astype(jnp.float32)
    return (projection, correction)


def solution(mesh):
    placed = (
        P("leaf", "blk", None),
        P("leaf", "blk", None),
        P("leaf", "blk"),
        P("leaf", None),
        P("leaf"),
        P("leaf"),
    )
    return jax.shard_map(
        per_device,
        mesh=mesh,
        in_specs=placed,
        out_specs=(P("leaf", None, "blk"), P("leaf", "blk")),
        check_vma=False,
    )
```

profile of v0, /device:TPU:0, one launch (start us, length us, event | category | flops | bytes accessed | tf_op | source)
XLA Modules:
  0.0 753.2 jit_solution(2265045415476198051)
XLA Ops:
  7.2 0.0 copy-start
  7.2 0.0 all-gather.2.cloned.1.call-start
  7.2 0.7 all-gather.2.cloned.1.call-update
  7.9 0.0 copy-start.6
  7.9 0.0 copy-start.7
  7.9 0.0 reduce-scatter.2.cloned.1.call-start
  8.0 0.4 copy-done
  8.4 7.8 %fusion.26 = f32[2,512,2048]{2,1,0:T(8,128)} fusion(bf16[2,512,512]{2,1,0:T(8,128)(2,1)S(1)} %copy-done, bf16[2,512,2048]{2,1,0:T(8,128)(2,1)} %param.8), kind=kOutput, calls=%fused_computation.43 | convolution fusion | flops 2147483648 | bytes 13631488 | tf_op jit(solution)/shard_map/srm,srq->smq/dot_general | solution.py:12
  16.2 0.0 copy-done.6
  16.2 0.6 fusion.25
  16.8 0.0 copy-done.7
  16.9 0.1 iota_compare_fusion
  16.9 0.6 compare_and_fusion
  17.5 1.9 fusion.18
  19.5 283.9 %all-reduce.1 = bf16[2,512,2048]{2,1,0:T(8,128)(2,1)} all-reduce(f32[2,512,2048]{2,1,0:T(8,128)} %fusion.26), channel_id=1, replica_groups=mesh['leaf'=32,'blk'=4] {'blk'}, use_global_device_ids=true, to_apply=%region_0.0 | all-reduce | flops 2097152 | bytes 12582912 | tf_op jit(solution)/shard_map/psum | solution.py:13
  303.3 34.4 %all-gather.2.cloned.1.call-done = bf16[16384,512]{1,0:T(8,128)(2,1)} async-done(((bf16[512,512]{1,0:T(8,128)(2,1)}), bf16[16384,512]{1,0:T(8,128)(2,1)}) %all-gather.2.cloned.1.call-update) | async-done | bytes 16777232 | tf_op jit(solution)/shard_map/all_gather | solution.py:17
  337.8 11.3 %fusion.24 = (bf16[8,1024,512]{2,1,0:T(8,128)(2,1)}, bf16[8,1024,512]{2,1,0:T(8,128)(2,1)}) fusion(bf16[8,2048,512]{2,1,0:T(8,128)(2,1)} %bitcast.10), kind=kLoop, calls=%fused_computation.41 | loop fusion | bytes 33554432 | tf_op jit(solution)/shard_map/gather | solution.py:19
  349.1 4.1 gather_fusion.1
  353.2 5.4 gather_fusion
  358.6 0.0 copy-start.2
  358.6 0.0 copy-start.8
  358.6 5.4 fusion.8
  364.0 0.0 copy-start.9
  364.0 1.0 copy-done.9
  364.9 0.0 copy-done.2
  364.9 0.0 copy-done.8
  364.9 3.2 fusion.2
  368.1 4.3 slice_bitcast_fusion.1
  372.4 71.3 %gather_fusion.2 = f32[16384,512]{1,0:T(8,128)} fusion(f32[2048,512]{1,0:T(8,128)} %get-tuple-element.5, s32[16384]{0:T(1024)S(1)} %fusion.20), kind=kCustom, calls=%fused_computation.clone | custom fusion | bytes 67174400 | tf_op jit(solution)/shard_map/jit(_take)/gather | solution.py:31
  443.7 0.0 copy-start.3
  443.7 0.0 copy-start.4
  443.7 0.0 copy-start.5
  443.7 71.2 %gather_fusion.3 = f32[16384,512]{1,0:T(8,128)} fusion(f32[2048,512]{1,0:T(8,128)} %get-tuple-element.6, s32[16384]{0:T(1024)S(1)} %fusion.20), kind=kCustom, calls=%fused_computation.1.clone | custom fusion | bytes 67174400 | tf_op jit(solution)/shard_map/jit(_take)/gather | solution.py:31
  514.9 0.0 copy-done.3
  514.9 0.0 copy-done.4
  514.9 0.0 copy-done.5
  514.9 27.3 %fusion.1 = bf16[16384,512]{1,0:T(8,128)(2,1)} fusion(f32[16384,512]{1,0:T(8,128)} %gather_fusion.3, f32[16384,512]{1,0:T(8,128)} %gather_fusion.2, pred[16384]{0:T(1024)(128)(4,1)S(1)} %copy-done.3, pred[16384]{0:T(1024)(128)(4,1)S(1)} %copy-done.4, pred[16384]{0:T(1024)(128)(4,1)S(1)} %copy-done.5), kind=kLoop, calls=%fused_computation.6 | loop fusion | flops 50331648 | bytes 83935232 | tf_op jit(solution)/shard_map/convert_element_type | solution.py:35
  542.2 0.0 copy-start.1
  542.2 0.0 reduce-scatter.2.cloned.1.call-update
  542.3 202.0 %reduce-scatter.2.cloned.1.call-done = bf16[512,512]{1,0:T(8,128)(2,1)} async-done(((bf16[16384,512]{1,0:T(8,128)(2,1)}), bf16[512,512]{1,0:T(8,128)(2,1)}) %reduce-scatter.2.cloned.1.call-update) | async-done | bytes 524304 | tf_op jit(solution)/shard_map/reduce_scatter | solution.py:34
  744.3 2.1 convert_element_type.23
  746.4 0.0 copy-done.1
  (3 shorter events, 0.0 us)
Async XLA Ops:
  7.2 1.2 copy-start
  7.2 330.6 %all-gather.2.cloned.1.call-start = ((), (), s32[]{:S(2)}) async-start(), calls=%async_computation.1 | async-start | bytes 17301504 | tf_op jit(solution)/shard_map/all_gather | solution.py:17
  7.9 8.3 %copy-start.6 = (s32[2]{0:T(128)S(1)}, s32[2]{0:T(128)}, u32[]{:S(2)}) copy-start(s32[2]{0:T(128)} %param.13) | copy-start | bytes 28
  7.9 8.9 %copy-start.7 = (s32[2]{0:T(128)S(1)}, s32[2]{0:T(128)}, u32[]{:S(2)}) copy-start(s32[2]{0:T(128)} %param.12) | copy-start | bytes 28
  7.9 736.3 %reduce-scatter.2.cloned.1.call-start = ((), (), s32[]{:S(2)}) async-start(), calls=%async_computation.2 | async-start | bytes 17301504 | tf_op jit(solution)/shard_map/reduce_scatter | solution.py:34
  358.6 6.3 copy-start.2
  358.6 6.4 copy-start.8
  364.0 1.0 copy-start.9
  443.7 71.2 %copy-start.3 = (pred[16384]{0:T(1024)(128)(4,1)S(1)}, pred[16384]{0:T(1024)(128)(4,1)}, u32[]{:S(2)}) copy-start(pred[16384]{0:T(1024)(128)(4,1)} %compare_and_fusion) | copy-start | bytes 49156
  443.7 71.2 %copy-start.4 = (pred[16384]{0:T(1024)(128)(4,1)S(1)}, pred[16384]{0:T(1024)(128)(4,1)}, u32[]{:S(2)}) copy-start(pred[16384]{0:T(1024)(128)(4,1)} %get-tuple-element.9) | copy-start | bytes 49156
  443.7 71.2 %copy-start.5 = (pred[16384]{0:T(1024)(128)(4,1)S(1)}, pred[16384]{0:T(1024)(128)(4,1)}, u32[]{:S(2)}) copy-start(pred[16384]{0:T(1024)(128)(4,1)} %get-tuple-element.10) | copy-start | bytes 49156
  542.2 204.2 %copy-start.1 = (bf16[2,512,512]{2,1,0:T(8,128)(2,1)S(1)}, bf16[2,512,512]{2,1,0:T(8,128)(2,1)}, u32[]{:S(2)}) copy-start(bf16[2,512,512]{2,1,0:T(8,128)(2,1)} %param.9) | copy-start | bytes 3145732
Sparse Core Ops, SparseCore 0:
  9.7 328.0 all-gather.1
  542.4 201.8 reduce-scatter.1
where the time goes:
time: 754 us; the launch traced here: 753 us
  blocking collectives  284 us (38%)
  waiting for transfers between devices  237 us (31%)
  local copies, waits for them, and re-layouts  170 us (23%)
  other arithmetic  32 us (4%)
  matrix products  16.3 us (2%)
  between operations  14.1 us (2%)
    psum x1, blocking collectives, per_device(): summed = lax.psum(partial_value, 'blk')  284 us
    reduce_scatter x1, waiting for transfers between devices, per_device(): lax.psum_scatter(total.astype(jnp.bfloat16), 'leaf', scatter_dimension=0,...  202 us
    gather x2, local copies, waits for them, and re-layouts, per_device(): taken = jnp.take(terms[index], within, axis=0)  143 us
    all_gather x1, waiting for transfers between devices, per_device(): every = lax.all_gather(basis, 'leaf', axis=0, tiled=True)  34.4 us
    convert_element_type x1, other arithmetic, per_device(): total.astype(jnp.bfloat16)  27.3 us
    gather x3, local copies, waits for them, and re-layouts, per_device(): picked = blocks[ancestry]  20.8 us
  transfers between devices with their start and end apart: 2, of which 2 were waited for; matrix products, arithmetic and copies ran while one was open for 1% of the time, Pallas kernels for 0%

commit v1 on v0

v1 whole, which is shorter than its diff:
```python
import jax
import jax.numpy as jnp
import numpy as np
from jax import lax
from jax.experimental import pallas as pl
from jax.experimental.pallas import tpu as pltpu
from jax.sharding import PartitionSpec as P

AXES = ("leaf", "blk")
SHAPE = (2, 4, 4, 2, 2)
ROWS = 400
LINES = 416
TILE = 512
WIDTHS = (256, 256)
BF = jnp.bfloat16
F32 = jnp.float32
VMEM = pl.BlockSpec(memory_space=pltpu.VMEM)
SMEM = pl.BlockSpec(memory_space=pltpu.SMEM)


def shift(value, xl=0, y=0, z=0, xh=0, c=0):
    pairs = []
    for spot in np.ndindex(*SHAPE):
        to = tuple((a + b) % n for a, b, n in zip(spot, (xl, y, z, xh, c), SHAPE))
        pairs.append((int(np.ravel_multi_index(spot, SHAPE)), int(np.ravel_multi_index(to, SHAPE))))
    return lax.ppermute(value, AXES, pairs)


def tdot(a, b):
    return lax.dot_general(a, b, (((0,), (0,)), ((), ())), preferred_element_type=F32)


def couple(which, spot, counts, ancestry, modes, stiffness):
    def side(spot):
        return spot[3] if which == 0 else 1 - spot[3]

    def kernel(spot, counts, ancestry, modes, stiffness, out, turned):
        @pl.when(pl.program_id(0) == 0)
        def _():
            turned[...] = modes[0].astype(F32).T[:ROWS].astype(BF)

        value = jnp.dot(turned[...], stiffness[0], preferred_element_type=F32)
        row = lax.broadcasted_iota(jnp.int32, value.shape, 0)
        out[0, pl.ds(0, ROWS)] = jnp.where(row < counts[side(spot)], value, 0.0).astype(BF)
        tag = jnp.zeros((LINES - ROWS, TILE), F32)
        if which == 0:
            row = lax.broadcasted_iota(jnp.int32, tag.shape, 0)
            for j in range(2):
                tag = jnp.where(row == j, ancestry[spot[3] ^ j].astype(F32), tag)
        out[0, pl.ds(ROWS, LINES - ROWS)] = tag.astype(BF)

    return pl.pallas_call(
        kernel,
        out_shape=jax.ShapeDtypeStruct((4, LINES, TILE), BF),
        grid_spec=pltpu.PrefetchScalarGridSpec(
            num_scalar_prefetch=3,
            grid=(4,),
            in_specs=[
                pl.BlockSpec((1, 512, 512), lambda d, spot, *_: (side(spot), 0, 0)),
                pl.BlockSpec((1, 512, TILE), lambda d, spot, *_: (side(spot), 0, (spot[2] + d) & 3)),
            ],
            out_specs=pl.BlockSpec((1, LINES, TILE), lambda d, *_: (d, 0, 0)),
            scratch_shapes=[pltpu.VMEM((ROWS, 512), BF)],
        ),
        compiler_params=pltpu.CompilerParams(vmem_limit_bytes=56 << 20),
        cost_estimate=pl.CostEstimate(flops=2 * 512 * 512 * 2048, bytes_accessed=4 << 20, transcendentals=0),
        name="couple",
    )(spot, counts, ancestry, modes, stiffness)


def relative(separator, spot):
    return ((separator >> 2) ^ spot[0]) * 4 + ((separator - spot[1]) & 3)


def ancestor(own, j):
    tag = own[pl.ds(ROWS, LINES - ROWS), pl.ds(0, 128)].astype(F32)
    row = lax.broadcasted_iota(jnp.int32, tag.shape, 0)
    return jnp.max(jnp.where(row == j, tag * 0.5, 0.0)).astype(jnp.int32)


def project(spot, own, other, tiles):
    def kernel(spot, own, other, *refs):
        tiles, out, held = refs[:8], refs[8], refs[9]
        for j, side in enumerate((own, other)):
            place = relative(ancestor(own, j), spot)
            for k in range(8):

                @pl.when(place == k)
                def _():
                    held[...] = tiles[k][...]

            out[j] = jnp.dot(side[pl.ds(0, ROWS)], held[...], preferred_element_type=F32).astype(BF)

    return pl.pallas_call(
        kernel,
        out_shape=jax.ShapeDtypeStruct((2, ROWS, TILE), BF),
        in_specs=[SMEM] + [VMEM] * 10,
        out_specs=VMEM,
        scratch_shapes=[pltpu.VMEM((TILE, TILE), BF)],
        compiler_params=pltpu.CompilerParams(vmem_limit_bytes=16 << 20),
        cost_estimate=pl.CostEstimate(flops=4 * ROWS * 512 * 512, bytes_accessed=3 << 20, transcendentals=0),
        name="project",
    )(spot, own, other, *tiles)


def finish(spot, eigen, parts):
    def kernel(spot, eigen, *refs):
        parts, projection, outs = refs[:4], refs[4], refs[5:]
        for j in range(2):
            side = spot[3] ^ j
            value = sum(part[j].astype(F32) for part in parts)
            projection[side, pl.ds(0, ROWS)] = value.astype(BF)
            projection[side, pl.ds(ROWS, 512 - ROWS)] = jnp.zeros((512 - ROWS, TILE), BF)
            scaled = (value / eigen[side, pl.ds(0, ROWS)]).astype(BF)
            first = 0
            for out, width in zip(outs, WIDTHS):
                out[j] = scaled[:, first : first + width]
                first += width

    return pl.pallas_call(
        kernel,
        out_shape=[jax.ShapeDtypeStruct((2, 512, TILE), BF)]
        + [jax.ShapeDtypeStruct((2, ROWS, width), BF) for width in WIDTHS],
        in_specs=[SMEM] + [VMEM] * 5,
        out_specs=[VMEM] * (1 + len(WIDTHS)),
        compiler_params=pltpu.CompilerParams(vmem_limit_bytes=24 << 20),
        cost_estimate=pl.CostEstimate(flops=8 * ROWS * 512, bytes_accessed=5 << 20, transcendentals=0),
        name="finish",
    )(spot, eigen, *parts)


def correct(spot, coupled, scaled):
    width = scaled[0].shape[2]

    def kernel(spot, *refs):
        coupled, scaled, outs, total = refs[:8], refs[8:12], refs[12:16], refs[16]
        total[...] = jnp.zeros_like(total)
        for d in range(4):
            for j in range(2):
                place = relative(ancestor(coupled[2 * d], j), spot)
                total[place] += tdot(coupled[2 * d + j][pl.ds(0, ROWS)], scaled[d][j])
        for k in range(8):
            outs[k % 4][k // 4] = total[k].astype(BF)

    return pl.pallas_call(
        kernel,
        out_shape=[jax.ShapeDtypeStruct((2, TILE, width), BF)] * 4,
        in_specs=[SMEM] + [VMEM] * 12,
        out_specs=[VMEM] * 4,
        scratch_shapes=[pltpu.VMEM((8, TILE, width), F32)],
        compiler_params=pltpu.CompilerParams(vmem_limit_bytes=32 << 20),
        cost_estimate=pl.CostEstimate(flops=16 * ROWS * 512 * width, bytes_accessed=8 << 20, transcendentals=0),
        name="correct",
    )(spot, *coupled, *scaled)


def per_device(stiffness, modes, basis, eigen, counts, ancestry):
    leaf, blk = lax.axis_index("leaf"), lax.axis_index("blk")
    spot = jnp.stack([leaf >> 4, (leaf >> 2) & 3, leaf & 3, blk & 1])

    away = couple(1, spot, counts, ancestry, modes, stiffness)
    came = shift(away, c=1)
    crossed = shift(basis, xl=1)
    above, below = shift(basis, y=-1), shift(basis, y=1)
    kept = couple(0, spot, counts, ancestry, modes, stiffness)
    both = [(kept[d].astype(F32) + came[d].astype(F32)).astype(BF) for d in range(4)]
    half = {d: shift(both[d], z=d) if d else both[0] for d in (0, 2, 1, 3)}
    own, other, parts = {}, {}, {}

    def meet(d, extra):
        met = shift(half[d], xh=1)
        met, *extra = lax.optimization_barrier((met, *extra))
        own[d] = (half[d].astype(F32) + met.astype(F32)).astype(BF)
        other[d] = shift(own[d], c=1)
        return extra

    crossed, above, below = meet(0, (crossed, above, below))
    cabove, cbelow = shift(crossed, y=-1), shift(crossed, y=1)
    cabove, cbelow = meet(2, (cabove, cbelow))
    mid = TILE // 2
    far1 = shift(jnp.stack([above[:mid], cabove[:mid]]), y=-1)
    far2 = shift(jnp.stack([below[mid:], cbelow[mid:]]), y=1)
    far1, far2 = meet(1, (far1, far2))
    meet(3, ())
    far = jnp.concatenate([far1, far2], axis=1)
    tiles = [basis, above, far[0], below, crossed, cabove, far[1], cbelow]
    for d in (0, 2, 1, 3):
        part = project(spot, own[d], other[d], tiles)
        parts[d] = shift(part, z=-d) if d else part
    lam = eigen[:, :, None]
    projection, *scaled = finish(spot, lam, [parts[d] for d in range(4)])

    coupled = [item for d in range(4) for item in (own[d], other[d])]
    columns = []
    for piece in scaled:
        pieces = [piece] + [shift(piece, z=d) for d in (1, 2, 3)]
        terms = correct(spot, coupled, pieces)
        total = terms[0].astype(F32) + sum(shift(terms[k], y=k).astype(F32) for k in (2, 1, 3))
        columns.append(total[0] + shift(total[1].astype(BF), xl=1).astype(F32))
    return projection, jnp.concatenate(columns, axis=1)


def solution(mesh):
    placed = (
        P("leaf", "blk", None),
        P("leaf", "blk", None),
        P("leaf", "blk"),
        P("leaf", None),
        P("leaf"),
        P("leaf"),
    )
    return jax.shard_map(
        per_device,
        mesh=mesh,
        in_specs=placed,
        out_specs=(P("leaf", None, "blk"), P("leaf", "blk")),
        check_vma=False,
    )
```

time: 754 us -> 207 us (0.27)
  blocking collectives: 284 us -> 0 us
  local copies, waits for them, and re-layouts: 170 us -> 3.88 us
  waiting for transfers between devices: 237 us -> 114 us
  starting transfers between devices: 0.08 us -> 52.3 us
  Pallas kernels: 0 us -> 30.2 us
  other arithmetic: 32 us -> 5.53 us
  matrix products: 16.3 us -> 0 us
  between operations: 14.1 us -> 1.02 us
    psum x1 -> x0, blocking collectives: 284 us -> none  [per_device(): summed = lax.psum(partial_value, 'blk')]
    reduce_scatter x1 -> x0, waiting for transfers between devices: 202 us -> none  [per_device(): lax.psum_scatter(total.astype(jnp.bfloat16), 'leaf', scatter_dimension=0,...]
    gather x5 -> x0, local copies, waits for them, and re-layouts: 163 us -> none  [the longest x2 143 us: per_device(): taken = jnp.take(terms[index], within, axis=0)]
    ppermute x0 -> x36, waiting for transfers between devices: none -> 114 us  [shift(): return lax.ppermute(value, AXES, pairs)]
    ppermute x0 -> x36, starting transfers between devices: none -> 52.3 us  [shift(): return lax.ppermute(value, AXES, pairs)]
    all_gather x1 -> x0, waiting for transfers between devices: 34.4 us -> none  [per_device(): every = lax.all_gather(basis, 'leaf', axis=0, tiled=True)]
    pallas_call x0 -> x9, Pallas kernels: none -> 30.2 us  [the longest x2 11.1 us: couple(): pl.pallas_call(kernel, out_shape=jax.ShapeDtypeStruct((4, LINES, TILE), B...]
    convert_element_type x2 -> x5, other arithmetic: 29.4 us -> 3.07 us  [the longest x1 1.89 us: per_device(): (kept[d].astype(F32) + came[d].astype(F32)).astype(BF)]
  transfers between devices with their start and end apart: 2 -> 36, of which waited for: 2 -> 17; matrix products, arithmetic and copies ran while one was open for 1% -> 2% of each run, Pallas kernels for 0% -> 10%
where the time goes in v1:
time: 207 us
  waiting for transfers between devices  114 us (55%)
  starting transfers between devices  52.3 us (25%)
  Pallas kernels  30.2 us (15%)
  other arithmetic  5.53 us (3%)
  local copies, waits for them, and re-layouts  3.88 us (2%)
    ppermute x36, waiting for transfers between devices, shift(): return lax.ppermute(value, AXES, pairs)  114 us
    ppermute x36, starting transfers between devices, shift(): return lax.ppermute(value, AXES, pairs)  52.3 us
    pallas_call x2, Pallas kernels, couple(): pl.pallas_call(kernel, out_shape=jax.ShapeDtypeStruct((4, LINES, TILE), B...  11.1 us
    pallas_call x4, Pallas kernels, project(): pl.pallas_call(kernel, out_shape=jax.ShapeDtypeStruct((2, ROWS, TILE), BF...  9.55 us
    pallas_call x2, Pallas kernels, correct(): pl.pallas_call(kernel, out_shape=[jax.ShapeDtypeStruct((2, TILE, width),...  6.5 us
  transfers between devices with their start and end apart: 36, of which 17 were waited for; matrix products, arithmetic and copies ran while one was open for 2% of the time, Pallas kernels for 10%

profile of v1, /device:TPU:0, one launch (start us, length us, event | category | flops | bytes accessed | tf_op | source)
XLA Modules:
  0.0 206.6 jit_solution(16727066014545515624)
XLA Ops:
  0.6 0.6 pad_add_fusion.spot
  1.3 5.6 %couple.3 = bf16[4,416,512]{2,1,0:T(8,128)(2,1)} custom-call(s32[4]{0:T(128)} %pad_add_fusion.spot, s32[2]{0:T(128)} %counts.3, s32[2]{0:T(128)} %ancestry.3, bf16[2,512,512]{2,1,0:T(8,128)(2,1)} %modes.3, bf16[2,512,2048]{2,1,0:T(8,128)(2,1)} %stiffness.3), custom_call_target="tpu_custom_call" | custom-call | flops 1073741824 | bytes 4194304 | tf_op jit(solution)/shard_map/couple/pallas_call | solution.py:52
  6.9 1.6 collective-permute-start.2
  8.5 3.0 %collective-permute-start.3 = (bf16[512,512]{1,0:T(8,128)(2,1)S(1)}, bf16[512,512]{1,0:T(8,128)(2,1)S(1)}, u32[]{:S(2)}, u32[]{:S(2)}) collective-permute-start(bf16[512,512]{1,0:T(8,128)(2,1)S(1)} %copy-done), channel_id=1, source_target_pairs={{0,48},{1,49},{2,50},{3,51},{4,52},{5,53},{6,54},{7,55},{8,56},{9,... | collective-permute-start | bytes 1572872 | tf_op jit(solution)/shard_map/ppermute | solution.py:26
  11.6 5.5 %couple.2 = bf16[4,416,512]{2,1,0:T(8,128)(2,1)} custom-call(s32[4]{0:T(128)} %pad_add_fusion.spot, s32[2]{0:T(128)} %counts.3, s32[2]{0:T(128)} %ancestry.3, bf16[2,512,512]{2,1,0:T(8,128)(2,1)} %modes.3, bf16[2,512,2048]{2,1,0:T(8,128)(2,1)} %stiffness.3), custom_call_target="tpu_custom_call" | custom-call | flops 1073741824 | bytes 4194304 | tf_op jit(solution)/shard_map/couple/pallas_call | solution.py:52
  17.0 1.9 fusion.5
  18.9 2.8 %collective-permute-start.1 = (bf16[416,512]{1,0:T(8,128)(2,1)S(1)}, bf16[416,512]{1,0:T(8,128)(2,1)S(1)}, u32[]{:S(2)}, u32[]{:S(2)}) collective-permute-start(bf16[416,512]{1,0:T(8,128)(2,1)S(1)} %get-tuple-element.47), channel_id=1, source_target_pairs={{0,2},{1,3},{2,0},{3,1},{4,6},{5,7},{6,4},{7,5},{8,10},{9,11},{10,... | collective-permute-start | bytes 1277960 | tf_op jit(solution)/shard_map/ppermute | solution.py:26
  21.7 3.9 %collective-permute-start.8 = (bf16[416,512]{1,0:T(8,128)(2,1)S(1)}, bf16[416,512]{1,0:T(8,128)(2,1)S(1)}, u32[]{:S(2)}, u32[]{:S(2)}) collective-permute-start(bf16[416,512]{1,0:T(8,128)(2,1)S(1)} %get-tuple-element.45), channel_id=1, source_target_pairs={{0,8},{1,9},{2,10},{3,11},{4,12},{5,13},{6,14},{7,15},{8,0},{9,1},... | collective-permute-start | bytes 1277960 | tf_op jit(solution)/shard_map/ppermute | solution.py:26
  25.6 0.7 collective-permute-start.18
  26.3 0.1 collective-permute-done.4.refs_3_
  26.5 6.2 %collective-permute-done.1 = bf16[416,512]{1,0:T(8,128)(2,1)S(1)} collective-permute-done((bf16[416,512]{1,0:T(8,128)(2,1)S(1)}, bf16[416,512]{1,0:T(8,128)(2,1)S(1)}, u32[]{:S(2)}, u32[]{:S(2)}) %collective-permute-start.1) | collective-permute-done | bytes 426016 | tf_op jit(solution)/shard_map/ppermute | solution.py:26
  32.6 3.0 %collective-permute-start.10 = (bf16[512,512]{1,0:T(8,128)(2,1)S(1)}, bf16[512,512]{1,0:T(8,128)(2,1)S(1)}, u32[]{:S(2)}, u32[]{:S(2)}) collective-permute-start(bf16[512,512]{1,0:T(8,128)(2,1)S(1)} %collective-permute-done.2.refs_4_), channel_id=1, source_target_pairs={{0,48},{1,49},{2,50},{3,51},{4,52},{5,53},{6,54},{7,55},{8,56},{9,... | collective-permute-start | bytes 1572872 | tf_op jit(solution)/shard_map/ppermute | solution.py:26
  35.7 1.9 collective-permute-start.6
  37.6 2.2 %collective-permute-start.9 = (bf16[416,512]{1,0:T(8,128)(2,1)S(1)}, bf16[416,512]{1,0:T(8,128)(2,1)S(1)}, u32[]{:S(2)}, u32[]{:S(2)}) collective-permute-start(bf16[416,512]{1,0:T(8,128)(2,1)S(1)} %collective-permute-done.8), channel_id=1, source_target_pairs={{0,2},{1,3},{2,0},{3,1},{4,6},{5,7},{6,4},{7,5},{8,10},{9,11},{10,... | collective-permute-start | bytes 1277960 | tf_op jit(solution)/shard_map/ppermute | solution.py:26
  39.7 5.4 %collective-permute-done.18 = bf16[416,512]{1,0:T(8,128)(2,1)S(1)} collective-permute-done((bf16[416,512]{1,0:T(8,128)(2,1)S(1)}, bf16[416,512]{1,0:T(8,128)(2,1)S(1)}, u32[]{:S(2)}, u32[]{:S(2)}) %collective-permute-start.18) | collective-permute-done | bytes 426016 | tf_op jit(solution)/shard_map/ppermute | solution.py:26
  45.1 0.8 collective-permute-start.19
  46.0 4.8 %collective-permute-done.9 = bf16[416,512]{1,0:T(8,128)(2,1)S(1)} collective-permute-done((bf16[416,512]{1,0:T(8,128)(2,1)S(1)}, bf16[416,512]{1,0:T(8,128)(2,1)S(1)}, u32[]{:S(2)}, u32[]{:S(2)}) %collective-permute-start.9) | collective-permute-done | bytes 426016 | tf_op jit(solution)/shard_map/ppermute | solution.py:26
  50.9 1.2 collective-permute-start.13
  52.1 2.2 %collective-permute-start.12 = (bf16[2,256,512]{2,1,0:T(8,128)(2,1)S(1)}, bf16[2,256,512]{2,1,0:T(8,128)(2,1)S(1)}, u32[]{:S(2)}, u32[]{:S(2)}) collective-permute-start(bf16[2,256,512]{2,1,0:T(8,128)(2,1)S(1)} %pad_maximum_fusion.1), channel_id=1, source_target_pairs={{0,48},{1,49},{2,50},{3,51},{4,52},{5,53},{6,54},{7,55},{8,56},{9,... | collective-permute-start | bytes 1572872 | tf_op jit(solution)/shard_map/ppermute | solution.py:26
  54.3 2.4 %collective-permute-start.7 = (bf16[416,512]{1,0:T(8,128)(2,1)S(1)}, bf16[416,512]{1,0:T(8,128)(2,1)S(1)}, u32[]{:S(2)}, u32[]{:S(2)}) collective-permute-start(bf16[416,512]{1,0:T(8,128)(2,1)S(1)} %collective-permute-done.6), channel_id=1, source_target_pairs={{0,2},{1,3},{2,0},{3,1},{4,6},{5,7},{6,4},{7,5},{8,10},{9,11},{10,... | collective-permute-start | bytes 1277960 | tf_op jit(solution)/shard_map/ppermute | solution.py:26
  56.7 3.2 %collective-permute-done.19 = bf16[416,512]{1,0:T(8,128)(2,1)S(1)} collective-permute-done((bf16[416,512]{1,0:T(8,128)(2,1)S(1)}, bf16[416,512]{1,0:T(8,128)(2,1)S(1)}, u32[]{:S(2)}, u32[]{:S(2)}) %collective-permute-start.19) | collective-permute-done | bytes 426016 | tf_op jit(solution)/shard_map/ppermute | solution.py:26
  60.1 0.1 add_convert_fusion.2.own.refs_4_
  60.3 0.6 collective-permute-start.16
  60.8 6.9 %collective-permute-done.7 = bf16[416,512]{1,0:T(8,128)(2,1)S(1)} collective-permute-done((bf16[416,512]{1,0:T(8,128)(2,1)S(1)}, bf16[416,512]{1,0:T(8,128)(2,1)S(1)}, u32[]{:S(2)}, u32[]{:S(2)}) %collective-permute-start.7) | collective-permute-done | bytes 426016 | tf_op jit(solution)/shard_map/ppermute | solution.py:26
  68.2 0.4 copy-done.17
  68.6 2.4 %project.7 = bf16[2,400,512]{2,1,0:T(8,128)(2,1)} custom-call(s32[4]{0:T(128)S(1)} %copy-done.17, bf16[416,512]{1,0:T(8,128)(2,1)S(1)} %add_convert_fusion.own.refs_6_, bf16[416,512]{1,0:T(8,128)(2,1)S(1)} %collective-permute-done.20.other.refs_7_, bf16[512,512]{1,0:T(8,128)(2,1)S(1)} %copy-done, bf16[512,512]{1,0:T(8,128)(2,1)S(1)} %collective-permute-done.3.refs_1_, ...), custom_call_target="tpu_custom_call" | custom-call | flops 419430400 | bytes 3145728 | tf_op jit(solution)/shard_map/project/pallas_call | solution.py:94
  71.0 1.9 collective-permute-start.21
  73.0 2.4 %project.6 = bf16[2,400,512]{2,1,0:T(8,128)(2,1)} custom-call(s32[4]{0:T(128)S(1)} %copy-done.17, bf16[416,512]{1,0:T(8,128)(2,1)S(1)} %add_convert_fusion.2.own.refs_4_, bf16[416,512]{1,0:T(8,128)(2,1)S(1)} %collective-permute-done.16.other.refs_5_, bf16[512,512]{1,0:T(8,128)(2,1)S(1)} %copy-done, bf16[512,512]{1,0:T(8,128)(2,1)S(1)} %collective-permute-done.3.refs_1_, ...), custom_call_target="tpu_custom_call" | custom-call | flops 419430400 | bytes 3145728 | tf_op jit(solution)/shard_map/project/pallas_call | solution.py:94
  75.4 2.0 collective-permute-start.17
  77.5 2.4 %project.5 = bf16[2,400,512]{2,1,0:T(8,128)(2,1)} custom-call(s32[4]{0:T(128)S(1)} %copy-done.17, bf16[416,512]{1,0:T(8,128)(2,1)S(1)} %add_convert_fusion.3.own.refs_2_, bf16[416,512]{1,0:T(8,128)(2,1)S(1)} %collective-permute-done.14.other.refs_3_, bf16[512,512]{1,0:T(8,128)(2,1)S(1)} %copy-done, bf16[512,512]{1,0:T(8,128)(2,1)S(1)} %collective-permute-done.3.refs_1_, ...), custom_call_target="tpu_custom_call" | custom-call | flops 419430400 | bytes 3145728 | tf_op jit(solution)/shard_map/project/pallas_call | solution.py:94
  79.9 2.3 %collective-permute-start.15 = (bf16[2,400,512]{2,1,0:T(8,128)(2,1)}, bf16[2,400,512]{2,1,0:T(8,128)(2,1)}, u32[]{:S(2)}, u32[]{:S(2)}) collective-permute-start(bf16[2,400,512]{2,1,0:T(8,128)(2,1)} %project.5), channel_id=1, source_target_pairs={{0,12},{1,13},{2,14},{3,15},{4,0},{5,1},{6,2},{7,3},{8,4},{9,5},{1... | collective-permute-start | bytes 2457608 | tf_op jit(solution)/shard_map/ppermute | solution.py:26
  82.2 0.9 add_convert_fusion.6.own.refs_0_
  83.1 1.0 copy.8.eigen
  84.1 1.1 collective-permute-done.5.other.refs_1_
  85.2 1.0 copy-done.1
  86.2 1.0 copy-done.3
  87.3 2.2 %project.4.refs_0_ = bf16[2,400,512]{2,1,0:T(8,128)(2,1)S(1)} custom-call(s32[4]{0:T(128)S(1)} %copy-done.17, bf16[416,512]{1,0:T(8,128)(2,1)} %add_convert_fusion.6.own.refs_0_, bf16[416,512]{1,0:T(8,128)(2,1)} %collective-permute-done.5.other.refs_1_, bf16[512,512]{1,0:T(8,128)(2,1)S(1)} %copy-done.1, bf16[512,512]{1,0:T(8,128)(2,1)S(1)} %collective-permute-done.3.refs_1_, ...), custom_call_target="tpu_custom_call" | custom-call | flops 419430400 | bytes 3145728 | tf_op jit(solution)/shard_map/project/pallas_call | solution.py:94
  89.5 3.4 %collective-permute-done.21.refs_3_ = bf16[2,400,512]{2,1,0:T(8,128)(2,1)} collective-permute-done((bf16[2,400,512]{2,1,0:T(8,128)(2,1)}, bf16[2,400,512]{2,1,0:T(8,128)(2,1)}, u32[]{:S(2)}, u32[]{:S(2)}) %collective-permute-start.21) | collective-permute-done | bytes 819232 | tf_op jit(solution)/shard_map/ppermute | solution.py:26
  93.0 18.1 %collective-permute-done.17.refs_2_ = bf16[2,400,512]{2,1,0:T(8,128)(2,1)} collective-permute-done((bf16[2,400,512]{2,1,0:T(8,128)(2,1)}, bf16[2,400,512]{2,1,0:T(8,128)(2,1)}, u32[]{:S(2)}, u32[]{:S(2)}) %collective-permute-start.17) | collective-permute-done | bytes 819232 | tf_op jit(solution)/shard_map/ppermute | solution.py:26
  111.1 2.4 %collective-permute-done.15.refs_1_ = bf16[2,400,512]{2,1,0:T(8,128)(2,1)} collective-permute-done((bf16[2,400,512]{2,1,0:T(8,128)(2,1)}, bf16[2,400,512]{2,1,0:T(8,128)(2,1)}, u32[]{:S(2)}, u32[]{:S(2)}) %collective-permute-start.15) | collective-permute-done | bytes 819232 | tf_op jit(solution)/shard_map/ppermute | solution.py:26
  113.5 3.1 %finish.1 = (bf16[2,512,512]{2,1,0:T(8,128)(2,1)}, bf16[2,400,256]{2,1,0:T(8,128)(2,1)S(1)}, bf16[2,400,256]{2,1,0:T(8,128)(2,1)S(1)}) custom-call(s32[4]{0:T(128)S(1)} %copy-done.17, f32[2,512,1]{2,1,0:T(8,128)S(1)} %copy-done.16, bf16[2,400,512]{2,1,0:T(8,128)(2,1)S(1)} %project.4.refs_0_, bf16[2,400,512]{2,1,0:T(8,128)(2,1)} %collective-permute-done.15.refs_1_, ...), custom_call_target="tpu_custom_call" | custom-call | flops 1638400 | bytes 5242880 | tf_op jit(solution)/shard_map/finish/pallas_call | solution.py:120
  116.6 2.9 %collective-permute-start.22 = (bf16[2,400,256]{2,1,0:T(8,128)(2,1)S(1)}, bf16[2,400,256]{2,1,0:T(8,128)(2,1)S(1)}, u32[]{:S(2)}, u32[]{:S(2)}) collective-permute-start(bf16[2,400,256]{2,1,0:T(8,128)(2,1)S(1)} %get-tuple-element.34.refs_8_), channel_id=1, source_target_pairs={{0,4},{1,5},{2,6},{3,7},{4,8},{5,9},{6,10},{7,11},{8,12},{9,13},{1... | collective-permute-start | bytes 1228808 | tf_op jit(solution)/shard_map/ppermute | solution.py:26
  119.5 1.2 collective-permute-start.23
  120.7 2.1 %collective-permute-start.24 = (bf16[2,400,256]{2,1,0:T(8,128)(2,1)S(1)}, bf16[2,400,256]{2,1,0:T(8,128)(2,1)S(1)}, u32[]{:S(2)}, u32[]{:S(2)}) collective-permute-start(bf16[2,400,256]{2,1,0:T(8,128)(2,1)S(1)} %get-tuple-element.34.refs_8_), channel_id=1, source_target_pairs={{0,12},{1,13},{2,14},{3,15},{4,0},{5,1},{6,2},{7,3},{8,4},{9,5},{1... | collective-permute-start | bytes 1228808 | tf_op jit(solution)/shard_map/ppermute | solution.py:26
  122.8 15.3 %collective-permute-done.22.refs_9_ = bf16[2,400,256]{2,1,0:T(8,128)(2,1)S(1)} collective-permute-done((bf16[2,400,256]{2,1,0:T(8,128)(2,1)S(1)}, bf16[2,400,256]{2,1,0:T(8,128)(2,1)S(1)}, u32[]{:S(2)}, u32[]{:S(2)}) %collective-permute-start.22) | collective-permute-done | bytes 409632 | tf_op jit(solution)/shard_map/ppermute | solution.py:26
  138.1 1.7 collective-permute-done.23.refs_10_
  139.8 3.3 %correct.2 = (bf16[2,512,256]{2,1,0:T(8,128)(2,1)S(1)}, bf16[2,512,256]{2,1,0:T(8,128)(2,1)S(1)}, bf16[2,512,256]{2,1,0:T(8,128)(2,1)S(1)}, bf16[2,512,256]{2,1,0:T(8,128)(2,1)S(1)}) custom-call(s32[4]{0:T(128)S(1)} %copy-done.17, bf16[416,512]{1,0:T(8,128)(2,1)} %add_convert_fusion.6.own.refs_0_, bf16[416,512]{1,0:T(8,128)(2,1)} %collective-permute-done.5.other.refs_1_, ...), custom_call_target="tpu_custom_call" | custom-call | flops 838860800 | bytes 8388608 | tf_op jit(solution)/shard_map/correct/pallas_call | solution.py:145
  143.1 2.4 %collective-permute-start.25 = (bf16[2,512,256]{2,1,0:T(8,128)(2,1)S(1)}, bf16[2,512,256]{2,1,0:T(8,128)(2,1)S(1)}, u32[]{:S(2)}, u32[]{:S(2)}) collective-permute-start(bf16[2,512,256]{2,1,0:T(8,128)(2,1)S(1)} %get-tuple-element.36), channel_id=1, source_target_pairs={{0,32},{1,33},{2,34},{3,35},{4,36},{5,37},{6,38},{7,39},{8,40},{9,... | collective-permute-start | bytes 1572872 | tf_op jit(solution)/shard_map/ppermute | solution.py:26
  145.5 1.5 collective-permute-start.26
  147.0 1.8 collective-permute-start.27
  148.8 2.4 %collective-permute-start.30 = (bf16[2,400,256]{2,1,0:T(8,128)(2,1)S(1)}, bf16[2,400,256]{2,1,0:T(8,128)(2,1)S(1)}, u32[]{:S(2)}, u32[]{:S(2)}) collective-permute-start(bf16[2,400,256]{2,1,0:T(8,128)(2,1)S(1)} %get-tuple-element.39.refs_8_), channel_id=1, source_target_pairs={{0,8},{1,9},{2,10},{3,11},{4,12},{5,13},{6,14},{7,15},{8,0},{9,1},... | collective-permute-start | bytes 1228808 | tf_op jit(solution)/shard_map/ppermute | solution.py:26
  151.1 1.4 collective-permute-start.31
  152.5 6.5 %collective-permute-done.30.refs_10_ = bf16[2,400,256]{2,1,0:T(8,128)(2,1)S(1)} collective-permute-done((bf16[2,400,256]{2,1,0:T(8,128)(2,1)S(1)}, bf16[2,400,256]{2,1,0:T(8,128)(2,1)S(1)}, u32[]{:S(2)}, u32[]{:S(2)}) %collective-permute-start.30) | collective-permute-done | bytes 409632 | tf_op jit(solution)/shard_map/ppermute | solution.py:26
  159.0 9.0 %collective-permute-done.31.refs_11_ = bf16[2,400,256]{2,1,0:T(8,128)(2,1)S(1)} collective-permute-done((bf16[2,400,256]{2,1,0:T(8,128)(2,1)S(1)}, bf16[2,400,256]{2,1,0:T(8,128)(2,1)S(1)}, u32[]{:S(2)}, u32[]{:S(2)}) %collective-permute-start.31) | collective-permute-done | bytes 409632 | tf_op jit(solution)/shard_map/ppermute | solution.py:26
  168.0 3.2 %correct.3 = (bf16[2,512,256]{2,1,0:T(8,128)(2,1)S(1)}, bf16[2,512,256]{2,1,0:T(8,128)(2,1)S(1)}, bf16[2,512,256]{2,1,0:T(8,128)(2,1)S(1)}, bf16[2,512,256]{2,1,0:T(8,128)(2,1)S(1)}) custom-call(s32[4]{0:T(128)S(1)} %copy-done.17, bf16[416,512]{1,0:T(8,128)(2,1)} %add_convert_fusion.6.own.refs_0_, bf16[416,512]{1,0:T(8,128)(2,1)} %collective-permute-done.5.other.refs_1_, ...), custom_call_target="tpu_custom_call" | custom-call | flops 838860800 | bytes 8388608 | tf_op jit(solution)/shard_map/correct/pallas_call | solution.py:145
  171.3 0.7 collective-permute-start.32
  171.9 0.5 collective-permute-start.33
  172.5 2.7 %collective-permute-start.34 = (bf16[2,512,256]{2,1,0:T(8,128)(2,1)S(1)}, bf16[2,512,256]{2,1,0:T(8,128)(2,1)S(1)}, u32[]{:S(2)}, u32[]{:S(2)}) collective-permute-start(bf16[2,512,256]{2,1,0:T(8,128)(2,1)S(1)} %get-tuple-element.43), channel_id=1, source_target_pairs={{0,48},{1,49},{2,50},{3,51},{4,52},{5,53},{6,54},{7,55},{8,56},{9,... | collective-permute-start | bytes 1572872 | tf_op jit(solution)/shard_map/ppermute | solution.py:26
  175.2 0.2 add_add_fusion.1
  175.6 12.2 %collective-permute-done.32 = bf16[2,512,256]{2,1,0:T(8,128)(2,1)S(1)} collective-permute-done((bf16[2,512,256]{2,1,0:T(8,128)(2,1)S(1)}, bf16[2,512,256]{2,1,0:T(8,128)(2,1)S(1)}, u32[]{:S(2)}, u32[]{:S(2)}) %collective-permute-start.32) | collective-permute-done | bytes 524320 | tf_op jit(solution)/shard_map/ppermute | solution.py:26
  187.7 9.2 %collective-permute-done.33 = bf16[2,512,256]{2,1,0:T(8,128)(2,1)S(1)} collective-permute-done((bf16[2,512,256]{2,1,0:T(8,128)(2,1)S(1)}, bf16[2,512,256]{2,1,0:T(8,128)(2,1)S(1)}, u32[]{:S(2)}, u32[]{:S(2)}) %collective-permute-start.33) | collective-permute-done | bytes 524320 | tf_op jit(solution)/shard_map/ppermute | solution.py:26
  196.9 0.2 add_add_fusion
  197.3 8.1 %collective-permute-done.35 = bf16[512,256]{1,0:T(8,128)(2,1)S(1)} collective-permute-done((bf16[512,256]{1,0:T(8,128)(2,1)S(1)}, bf16[512,256]{1,0:T(8,128)(2,1)S(1)}, u32[]{:S(2)}, u32[]{:S(2)}) %collective-permute-start.35) | collective-permute-done | bytes 262176 | tf_op jit(solution)/shard_map/ppermute | solution.py:26
  205.5 1.1 pad_maximum_fusion
  (78 shorter events, 1.2 us)
Async XLA Ops:
  1.3 5.6 %copy-start = (bf16[512,512]{1,0:T(8,128)(2,1)S(1)}, bf16[512,512]{1,0:T(8,128)(2,1)}, u32[]{:S(2)}) copy-start(bf16[512,512]{1,0:T(8,128)(2,1)} %refs_0_.7) | copy-start | bytes 1572868
  6.9 10.2 %collective-permute-start = (bf16[4,416,512]{2,1,0:T(8,128)(2,1)}, bf16[4,416,512]{2,1,0:T(8,128)(2,1)S(1)}, u32[]{:S(2)}, u32[]{:S(2)}) collective-permute-start(bf16[4,416,512]{2,1,0:T(8,128)(2,1)} %couple.3), channel_id=1, source_target_pairs={{0,1},{1,0},{2,3},{3,2},{4,5},{5,4},{6,7},{7,6},{8,9},{9,8},{10,11... | collective-permute-start | bytes 5111816 | tf_op jit(solution)/shard_map/ppermute | solution.py:26
  6.9 18.7 %collective-permute-start.2 = (bf16[512,512]{1,0:T(8,128)(2,1)S(1)}, bf16[512,512]{1,0:T(8,128)(2,1)S(1)}, u32[]{:S(2)}, u32[]{:S(2)}) collective-permute-start(bf16[512,512]{1,0:T(8,128)(2,1)S(1)} %copy-done), channel_id=1, source_target_pairs={{0,64},{1,65},{2,66},{3,67},{4,68},{5,69},{6,70},{7,71},{8,72},{9,... | collective-permute-start | bytes 1572872 | tf_op jit(solution)/shard_map/ppermute | solution.py:26
  8.5 17.8 %collective-permute-start.3 = (bf16[512,512]{1,0:T(8,128)(2,1)S(1)}, bf16[512,512]{1,0:T(8,128)(2,1)S(1)}, u32[]{:S(2)}, u32[]{:S(2)}) collective-permute-start(bf16[512,512]{1,0:T(8,128)(2,1)S(1)} %copy-done), channel_id=1, source_target_pairs={{0,48},{1,49},{2,50},{3,51},{4,52},{5,53},{6,54},{7,55},{8,56},{9,... | collective-permute-start | bytes 1572872 | tf_op jit(solution)/shard_map/ppermute | solution.py:26
  11.5 14.9 %collective-permute-start.4 = (bf16[512,512]{1,0:T(8,128)(2,1)S(1)}, bf16[512,512]{1,0:T(8,128)(2,1)S(1)}, u32[]{:S(2)}, u32[]{:S(2)}) collective-permute-start(bf16[512,512]{1,0:T(8,128)(2,1)S(1)} %copy-done), channel_id=1, source_target_pairs={{0,16},{1,17},{2,18},{3,19},{4,20},{5,21},{6,22},{7,23},{8,24},{9,... | collective-permute-start | bytes 1572872 | tf_op jit(solution)/shard_map/ppermute | solution.py:26
  18.9 13.7 %collective-permute-start.1 = (bf16[416,512]{1,0:T(8,128)(2,1)S(1)}, bf16[416,512]{1,0:T(8,128)(2,1)S(1)}, u32[]{:S(2)}, u32[]{:S(2)}) collective-permute-start(bf16[416,512]{1,0:T(8,128)(2,1)S(1)} %get-tuple-element.47), channel_id=1, source_target_pairs={{0,2},{1,3},{2,0},{3,1},{4,6},{5,7},{6,4},{7,5},{8,10},{9,11},{10,... | collective-permute-start | bytes 1277960 | tf_op jit(solution)/shard_map/ppermute | solution.py:26
  21.7 15.8 %collective-permute-start.8 = (bf16[416,512]{1,0:T(8,128)(2,1)S(1)}, bf16[416,512]{1,0:T(8,128)(2,1)S(1)}, u32[]{:S(2)}, u32[]{:S(2)}) collective-permute-start(bf16[416,512]{1,0:T(8,128)(2,1)S(1)} %get-tuple-element.45), channel_id=1, source_target_pairs={{0,8},{1,9},{2,10},{3,11},{4,12},{5,13},{6,14},{7,15},{8,0},{9,1},... | collective-permute-start | bytes 1277960 | tf_op jit(solution)/shard_map/ppermute | solution.py:26
  25.6 51.8 %copy-start.2 = (bf16[512,512]{1,0:T(8,128)(2,1)}, bf16[512,512]{1,0:T(8,128)(2,1)S(1)}, u32[]{:S(2)}) copy-start(bf16[512,512]{1,0:T(8,128)(2,1)S(1)} %collective-permute-done.2.refs_4_) | copy-start | bytes 1572868
  25.6 19.5 %collective-permute-start.18 = (bf16[416,512]{1,0:T(8,128)(2,1)S(1)}, bf16[416,512]{1,0:T(8,128)(2,1)S(1)}, u32[]{:S(2)}, u32[]{:S(2)}) collective-permute-start(bf16[416,512]{1,0:T(8,128)(2,1)S(1)} %get-tuple-element.44), channel_id=1, source_target_pairs={{0,12},{1,13},{2,14},{3,15},{4,0},{5,1},{6,2},{7,3},{8,4},{9,5},{1... | collective-permute-start | bytes 1277960 | tf_op jit(solution)/shard_map/ppermute | solution.py:26
  32.6 18.2 %collective-permute-start.10 = (bf16[512,512]{1,0:T(8,128)(2,1)S(1)}, bf16[512,512]{1,0:T(8,128)(2,1)S(1)}, u32[]{:S(2)}, u32[]{:S(2)}) collective-permute-start(bf16[512,512]{1,0:T(8,128)(2,1)S(1)} %collective-permute-done.2.refs_4_), channel_id=1, source_target_pairs={{0,48},{1,49},{2,50},{3,51},{4,52},{5,53},{6,54},{7,55},{8,56},{9,... | collective-permute-start | bytes 1572872 | tf_op jit(solution)/shard_map/ppermute | solution.py:26
  35.7 15.1 %collective-permute-start.11 = (bf16[512,512]{1,0:T(8,128)(2,1)S(1)}, bf16[512,512]{1,0:T(8,128)(2,1)S(1)}, u32[]{:S(2)}, u32[]{:S(2)}) collective-permute-start(bf16[512,512]{1,0:T(8,128)(2,1)S(1)} %collective-permute-done.2.refs_4_), channel_id=1, source_target_pairs={{0,16},{1,17},{2,18},{3,19},{4,20},{5,21},{6,22},{7,23},{8,24},{9,... | collective-permute-start | bytes 1572872 | tf_op jit(solution)/shard_map/ppermute | solution.py:26
  35.7 18.7 %collective-permute-start.6 = (bf16[416,512]{1,0:T(8,128)(2,1)S(1)}, bf16[416,512]{1,0:T(8,128)(2,1)S(1)}, u32[]{:S(2)}, u32[]{:S(2)}) collective-permute-start(bf16[416,512]{1,0:T(8,128)(2,1)S(1)} %get-tuple-element.46), channel_id=1, source_target_pairs={{0,4},{1,5},{2,6},{3,7},{4,8},{5,9},{6,10},{7,11},{8,12},{9,13},{1... | collective-permute-start | bytes 1277960 | tf_op jit(solution)/shard_map/ppermute | solution.py:26
  37.6 13.2 %collective-permute-start.9 = (bf16[416,512]{1,0:T(8,128)(2,1)S(1)}, bf16[416,512]{1,0:T(8,128)(2,1)S(1)}, u32[]{:S(2)}, u32[]{:S(2)}) collective-permute-start(bf16[416,512]{1,0:T(8,128)(2,1)S(1)} %collective-permute-done.8), channel_id=1, source_target_pairs={{0,2},{1,3},{2,0},{3,1},{4,6},{5,7},{6,4},{7,5},{8,10},{9,11},{10,... | collective-permute-start | bytes 1277960 | tf_op jit(solution)/shard_map/ppermute | solution.py:26
  45.1 14.8 %collective-permute-start.19 = (bf16[416,512]{1,0:T(8,128)(2,1)S(1)}, bf16[416,512]{1,0:T(8,128)(2,1)S(1)}, u32[]{:S(2)}, u32[]{:S(2)}) collective-permute-start(bf16[416,512]{1,0:T(8,128)(2,1)S(1)} %collective-permute-done.18), channel_id=1, source_target_pairs={{0,2},{1,3},{2,0},{3,1},{4,6},{5,7},{6,4},{7,5},{8,10},{9,11},{10,... | collective-permute-start | bytes 1277960 | tf_op jit(solution)/shard_map/ppermute | solution.py:26
  50.9 16.9 %collective-permute-start.13 = (bf16[2,256,512]{2,1,0:T(8,128)(2,1)S(1)}, bf16[2,256,512]{2,1,0:T(8,128)(2,1)S(1)}, u32[]{:S(2)}, u32[]{:S(2)}) collective-permute-start(bf16[2,256,512]{2,1,0:T(8,128)(2,1)S(1)} %pad_maximum_fusion.2), channel_id=1, source_target_pairs={{0,16},{1,17},{2,18},{3,19},{4,20},{5,21},{6,22},{7,23},{8,24},{9,... | collective-permute-start | bytes 1572872 | tf_op jit(solution)/shard_map/ppermute | solution.py:26
  52.1 15.6 %collective-permute-start.12 = (bf16[2,256,512]{2,1,0:T(8,128)(2,1)S(1)}, bf16[2,256,512]{2,1,0:T(8,128)(2,1)S(1)}, u32[]{:S(2)}, u32[]{:S(2)}) collective-permute-start(bf16[2,256,512]{2,1,0:T(8,128)(2,1)S(1)} %pad_maximum_fusion.1), channel_id=1, source_target_pairs={{0,48},{1,49},{2,50},{3,51},{4,52},{5,53},{6,54},{7,55},{8,56},{9,... | collective-permute-start | bytes 1572872 | tf_op jit(solution)/shard_map/ppermute | solution.py:26
  54.3 13.4 %collective-permute-start.7 = (bf16[416,512]{1,0:T(8,128)(2,1)S(1)}, bf16[416,512]{1,0:T(8,128)(2,1)S(1)}, u32[]{:S(2)}, u32[]{:S(2)}) collective-permute-start(bf16[416,512]{1,0:T(8,128)(2,1)S(1)} %collective-permute-done.6), channel_id=1, source_target_pairs={{0,2},{1,3},{2,0},{3,1},{4,6},{5,7},{6,4},{7,5},{8,10},{9,11},{10,... | collective-permute-start | bytes 1277960 | tf_op jit(solution)/shard_map/ppermute | solution.py:26
  60.0 8.1 %copy-start.4 = (bf16[416,512]{1,0:T(8,128)(2,1)}, bf16[416,512]{1,0:T(8,128)(2,1)S(1)}, u32[]{:S(2)}) copy-start(bf16[416,512]{1,0:T(8,128)(2,1)S(1)} %add_convert_fusion.own.refs_6_) | copy-start | bytes 1277956
  60.0 8.1 %collective-permute-start.20 = (bf16[416,512]{1,0:T(8,128)(2,1)S(1)}, bf16[416,512]{1,0:T(8,128)(2,1)S(1)}, u32[]{:S(2)}, u32[]{:S(2)}) collective-permute-start(bf16[416,512]{1,0:T(8,128)(2,1)S(1)} %add_convert_fusion.own.refs_6_), channel_id=1, source_target_pairs={{0,1},{1,0},{2,3},{3,2},{4,5},{5,4},{6,7},{7,6},{8,9},{9,8},{10,11... | collective-permute-start | bytes 1277960 | tf_op jit(solution)/shard_map/ppermute | solution.py:26
  60.3 12.7 %copy-start.6 = (bf16[416,512]{1,0:T(8,128)(2,1)}, bf16[416,512]{1,0:T(8,128)(2,1)S(1)}, u32[]{:S(2)}) copy-start(bf16[416,512]{1,0:T(8,128)(2,1)S(1)} %add_convert_fusion.2.own.refs_4_) | copy-start | bytes 1277956
  60.3 12.7 %collective-permute-start.16 = (bf16[416,512]{1,0:T(8,128)(2,1)S(1)}, bf16[416,512]{1,0:T(8,128)(2,1)S(1)}, u32[]{:S(2)}, u32[]{:S(2)}) collective-permute-start(bf16[416,512]{1,0:T(8,128)(2,1)S(1)} %add_convert_fusion.2.own.refs_4_), channel_id=1, source_target_pairs={{0,1},{1,0},{2,3},{3,2},{4,5},{5,4},{6,7},{7,6},{8,9},{9,8},{10,11... | collective-permute-start | bytes 1277960 | tf_op jit(solution)/shard_map/ppermute | solution.py:26
  67.9 9.6 %copy-start.8 = (bf16[416,512]{1,0:T(8,128)(2,1)}, bf16[416,512]{1,0:T(8,128)(2,1)S(1)}, u32[]{:S(2)}) copy-start(bf16[416,512]{1,0:T(8,128)(2,1)S(1)} %add_convert_fusion.3.own.refs_2_) | copy-start | bytes 1277956
  67.9 0.7 copy-start.17
  67.9 9.5 %collective-permute-start.14 = (bf16[416,512]{1,0:T(8,128)(2,1)S(1)}, bf16[416,512]{1,0:T(8,128)(2,1)S(1)}, u32[]{:S(2)}, u32[]{:S(2)}) collective-permute-start(bf16[416,512]{1,0:T(8,128)(2,1)S(1)} %add_convert_fusion.3.own.refs_2_), channel_id=1, source_target_pairs={{0,1},{1,0},{2,3},{3,2},{4,5},{5,4},{6,7},{7,6},{8,9},{9,8},{10,11... | collective-permute-start | bytes 1277960 | tf_op jit(solution)/shard_map/ppermute | solution.py:26
  68.2 2.9 %copy-start.10 = (bf16[416,512]{1,0:T(8,128)(2,1)}, bf16[416,512]{1,0:T(8,128)(2,1)S(1)}, u32[]{:S(2)}) copy-start(bf16[416,512]{1,0:T(8,128)(2,1)S(1)} %collective-permute-done.20.other.refs_7_) | copy-start | bytes 1277956
  71.0 21.9 %collective-permute-start.21 = (bf16[2,400,512]{2,1,0:T(8,128)(2,1)}, bf16[2,400,512]{2,1,0:T(8,128)(2,1)}, u32[]{:S(2)}, u32[]{:S(2)}) collective-permute-start(bf16[2,400,512]{2,1,0:T(8,128)(2,1)} %project.7), channel_id=1, source_target_pairs={{0,4},{1,5},{2,6},{3,7},{4,8},{5,9},{6,10},{7,11},{8,12},{9,13},{1... | collective-permute-start | bytes 2457608 | tf_op jit(solution)/shard_map/ppermute | solution.py:26
  73.0 2.4 %copy-start.12 = (bf16[416,512]{1,0:T(8,128)(2,1)}, bf16[416,512]{1,0:T(8,128)(2,1)S(1)}, u32[]{:S(2)}) copy-start(bf16[416,512]{1,0:T(8,128)(2,1)S(1)} %collective-permute-done.16.other.refs_5_) | copy-start | bytes 1277956
  75.4 7.6 %copy-start.18 = (f32[2,512]{1,0:T(2,128)S(1)}, f32[2,512]{1,0:T(2,128)}, u32[]{:S(2)}) copy-start(f32[2,512]{1,0:T(2,128)} %param.9) | copy-start | bytes 12292
  75.4 35.7 %collective-permute-start.17 = (bf16[2,400,512]{2,1,0:T(8,128)(2,1)}, bf16[2,400,512]{2,1,0:T(8,128)(2,1)}, u32[]{:S(2)}, u32[]{:S(2)}) collective-permute-start(bf16[2,400,512]{2,1,0:T(8,128)(2,1)} %project.6), channel_id=1, source_target_pairs={{0,8},{1,9},{2,10},{3,11},{4,12},{5,13},{6,14},{7,15},{8,0},{9,1},... | collective-permute-start | bytes 2457608 | tf_op jit(solution)/shard_map/ppermute | solution.py:26
  77.5 2.5 %copy-start.14 = (bf16[416,512]{1,0:T(8,128)(2,1)}, bf16[416,512]{1,0:T(8,128)(2,1)S(1)}, u32[]{:S(2)}) copy-start(bf16[416,512]{1,0:T(8,128)(2,1)S(1)} %collective-permute-done.14.other.refs_3_) | copy-start | bytes 1277956
  79.9 33.5 %collective-permute-start.15 = (bf16[2,400,512]{2,1,0:T(8,128)(2,1)}, bf16[2,400,512]{2,1,0:T(8,128)(2,1)}, u32[]{:S(2)}, u32[]{:S(2)}) collective-permute-start(bf16[2,400,512]{2,1,0:T(8,128)(2,1)} %project.5), channel_id=1, source_target_pairs={{0,12},{1,13},{2,14},{3,15},{4,0},{5,1},{6,2},{7,3},{8,4},{9,5},{1... | collective-permute-start | bytes 2457608 | tf_op jit(solution)/shard_map/ppermute | solution.py:26
  83.1 2.1 %collective-permute-start.5 = (bf16[416,512]{1,0:T(8,128)(2,1)}, bf16[416,512]{1,0:T(8,128)(2,1)}, u32[]{:S(2)}, u32[]{:S(2)}) collective-permute-start(bf16[416,512]{1,0:T(8,128)(2,1)} %add_convert_fusion.6.own.refs_0_), channel_id=1, source_target_pairs={{0,1},{1,0},{2,3},{3,2},{4,5},{5,4},{6,7},{7,6},{8,9},{9,8},{10,11... | collective-permute-start | bytes 1277960 | tf_op jit(solution)/shard_map/ppermute | solution.py:26
  85.2 1.0 copy-start.1
  86.2 1.0 copy-start.3
  87.3 26.2 %copy-start.16 = (f32[2,512,1]{2,1,0:T(8,128)S(1)}, f32[2,512,1]{2,1,0:T(8,128)}, u32[]{:S(2)}) copy-start(f32[2,512,1]{2,1,0:T(8,128)} %copy.8.eigen) | copy-start | bytes 12292
  89.5 50.3 %copy-start.5 = (bf16[416,512]{1,0:T(8,128)(2,1)S(1)}, bf16[416,512]{1,0:T(8,128)(2,1)}, u32[]{:S(2)}) copy-start(bf16[416,512]{1,0:T(8,128)(2,1)} %copy-done.4) | copy-start | bytes 1277956
  89.5 50.3 %copy-start.7 = (bf16[416,512]{1,0:T(8,128)(2,1)S(1)}, bf16[416,512]{1,0:T(8,128)(2,1)}, u32[]{:S(2)}) copy-start(bf16[416,512]{1,0:T(8,128)(2,1)} %copy-done.6) | copy-start | bytes 1277956
  89.5 50.3 %copy-start.9 = (bf16[416,512]{1,0:T(8,128)(2,1)S(1)}, bf16[416,512]{1,0:T(8,128)(2,1)}, u32[]{:S(2)}) copy-start(bf16[416,512]{1,0:T(8,128)(2,1)} %copy-done.8) | copy-start | bytes 1277956
  89.5 50.3 %copy-start.11 = (bf16[416,512]{1,0:T(8,128)(2,1)S(1)}, bf16[416,512]{1,0:T(8,128)(2,1)}, u32[]{:S(2)}) copy-start(bf16[416,512]{1,0:T(8,128)(2,1)} %copy-done.10) | copy-start | bytes 1277956
  89.5 50.3 %copy-start.13 = (bf16[416,512]{1,0:T(8,128)(2,1)S(1)}, bf16[416,512]{1,0:T(8,128)(2,1)}, u32[]{:S(2)}) copy-start(bf16[416,512]{1,0:T(8,128)(2,1)} %copy-done.12) | copy-start | bytes 1277956
  89.5 50.3 %copy-start.15 = (bf16[416,512]{1,0:T(8,128)(2,1)S(1)}, bf16[416,512]{1,0:T(8,128)(2,1)}, u32[]{:S(2)}) copy-start(bf16[416,512]{1,0:T(8,128)(2,1)} %copy-done.14) | copy-start | bytes 1277956
  116.6 21.5 %collective-permute-start.22 = (bf16[2,400,256]{2,1,0:T(8,128)(2,1)S(1)}, bf16[2,400,256]{2,1,0:T(8,128)(2,1)S(1)}, u32[]{:S(2)}, u32[]{:S(2)}) collective-permute-start(bf16[2,400,256]{2,1,0:T(8,128)(2,1)S(1)} %get-tuple-element.34.refs_8_), channel_id=1, source_target_pairs={{0,4},{1,5},{2,6},{3,7},{4,8},{5,9},{6,10},{7,11},{8,12},{9,13},{1... | collective-permute-start | bytes 1228808 | tf_op jit(solution)/shard_map/ppermute | solution.py:26
  119.5 20.3 %collective-permute-start.23 = (bf16[2,400,256]{2,1,0:T(8,128)(2,1)S(1)}, bf16[2,400,256]{2,1,0:T(8,128)(2,1)S(1)}, u32[]{:S(2)}, u32[]{:S(2)}) collective-permute-start(bf16[2,400,256]{2,1,0:T(8,128)(2,1)S(1)} %get-tuple-element.34.refs_8_), channel_id=1, source_target_pairs={{0,8},{1,9},{2,10},{3,11},{4,12},{5,13},{6,14},{7,15},{8,0},{9,1},... | collective-permute-start | bytes 1228808 | tf_op jit(solution)/shard_map/ppermute | solution.py:26
  120.7 19.1 %collective-permute-start.24 = (bf16[2,400,256]{2,1,0:T(8,128)(2,1)S(1)}, bf16[2,400,256]{2,1,0:T(8,128)(2,1)S(1)}, u32[]{:S(2)}, u32[]{:S(2)}) collective-permute-start(bf16[2,400,256]{2,1,0:T(8,128)(2,1)S(1)} %get-tuple-element.34.refs_8_), channel_id=1, source_target_pairs={{0,12},{1,13},{2,14},{3,15},{4,0},{5,1},{6,2},{7,3},{8,4},{9,5},{1... | collective-permute-start | bytes 1228808 | tf_op jit(solution)/shard_map/ppermute | solution.py:26
  122.8 28.3 %collective-permute-start.29 = (bf16[2,400,256]{2,1,0:T(8,128)(2,1)S(1)}, bf16[2,400,256]{2,1,0:T(8,128)(2,1)S(1)}, u32[]{:S(2)}, u32[]{:S(2)}) collective-permute-start(bf16[2,400,256]{2,1,0:T(8,128)(2,1)S(1)} %get-tuple-element.39.refs_8_), channel_id=1, source_target_pairs={{0,4},{1,5},{2,6},{3,7},{4,8},{5,9},{6,10},{7,11},{8,12},{9,13},{1... | collective-permute-start | bytes 1228808 | tf_op jit(solution)/shard_map/ppermute | solution.py:26
  143.1 29.4 %collective-permute-start.25 = (bf16[2,512,256]{2,1,0:T(8,128)(2,1)S(1)}, bf16[2,512,256]{2,1,0:T(8,128)(2,1)S(1)}, u32[]{:S(2)}, u32[]{:S(2)}) collective-permute-start(bf16[2,512,256]{2,1,0:T(8,128)(2,1)S(1)} %get-tuple-element.36), channel_id=1, source_target_pairs={{0,32},{1,33},{2,34},{3,35},{4,36},{5,37},{6,38},{7,39},{8,40},{9,... | collective-permute-start | bytes 1572872 | tf_op jit(solution)/shard_map/ppermute | solution.py:26
  145.5 29.7 %collective-permute-start.26 = (bf16[2,512,256]{2,1,0:T(8,128)(2,1)S(1)}, bf16[2,512,256]{2,1,0:T(8,128)(2,1)S(1)}, u32[]{:S(2)}, u32[]{:S(2)}) collective-permute-start(bf16[2,512,256]{2,1,0:T(8,128)(2,1)S(1)} %get-tuple-element.37), channel_id=1, source_target_pairs={{0,16},{1,17},{2,18},{3,19},{4,20},{5,21},{6,22},{7,23},{8,24},{9,... | collective-permute-start | bytes 1572872 | tf_op jit(solution)/shard_map/ppermute | solution.py:26
  147.0 28.2 %collective-permute-start.27 = (bf16[2,512,256]{2,1,0:T(8,128)(2,1)S(1)}, bf16[2,512,256]{2,1,0:T(8,128)(2,1)S(1)}, u32[]{:S(2)}, u32[]{:S(2)}) collective-permute-start(bf16[2,512,256]{2,1,0:T(8,128)(2,1)S(1)} %get-tuple-element.38), channel_id=1, source_target_pairs={{0,48},{1,49},{2,50},{3,51},{4,52},{5,53},{6,54},{7,55},{8,56},{9,... | collective-permute-start | bytes 1572872 | tf_op jit(solution)/shard_map/ppermute | solution.py:26
  148.8 10.3 %collective-permute-start.30 = (bf16[2,400,256]{2,1,0:T(8,128)(2,1)S(1)}, bf16[2,400,256]{2,1,0:T(8,128)(2,1)S(1)}, u32[]{:S(2)}, u32[]{:S(2)}) collective-permute-start(bf16[2,400,256]{2,1,0:T(8,128)(2,1)S(1)} %get-tuple-element.39.refs_8_), channel_id=1, source_target_pairs={{0,8},{1,9},{2,10},{3,11},{4,12},{5,13},{6,14},{7,15},{8,0},{9,1},... | collective-permute-start | bytes 1228808 | tf_op jit(solution)/shard_map/ppermute | solution.py:26
  151.1 16.9 %collective-permute-start.31 = (bf16[2,400,256]{2,1,0:T(8,128)(2,1)S(1)}, bf16[2,400,256]{2,1,0:T(8,128)(2,1)S(1)}, u32[]{:S(2)}, u32[]{:S(2)}) collective-permute-start(bf16[2,400,256]{2,1,0:T(8,128)(2,1)S(1)} %get-tuple-element.39.refs_8_), channel_id=1, source_target_pairs={{0,12},{1,13},{2,14},{3,15},{4,0},{5,1},{6,2},{7,3},{8,4},{9,5},{1... | collective-permute-start | bytes 1228808 | tf_op jit(solution)/shard_map/ppermute | solution.py:26
  171.3 16.4 %collective-permute-start.32 = (bf16[2,512,256]{2,1,0:T(8,128)(2,1)S(1)}, bf16[2,512,256]{2,1,0:T(8,128)(2,1)S(1)}, u32[]{:S(2)}, u32[]{:S(2)}) collective-permute-start(bf16[2,512,256]{2,1,0:T(8,128)(2,1)S(1)} %get-tuple-element.41), channel_id=1, source_target_pairs={{0,32},{1,33},{2,34},{3,35},{4,36},{5,37},{6,38},{7,39},{8,40},{9,... | collective-permute-start | bytes 1572872 | tf_op jit(solution)/shard_map/ppermute | solution.py:26
  171.9 24.9 %collective-permute-start.33 = (bf16[2,512,256]{2,1,0:T(8,128)(2,1)S(1)}, bf16[2,512,256]{2,1,0:T(8,128)(2,1)S(1)}, u32[]{:S(2)}, u32[]{:S(2)}) collective-permute-start(bf16[2,512,256]{2,1,0:T(8,128)(2,1)S(1)} %get-tuple-element.42), channel_id=1, source_target_pairs={{0,16},{1,17},{2,18},{3,19},{4,20},{5,21},{6,22},{7,23},{8,24},{9,... | collective-permute-start | bytes 1572872 | tf_op jit(solution)/shard_map/ppermute | solution.py:26
  172.5 24.4 %collective-permute-start.34 = (bf16[2,512,256]{2,1,0:T(8,128)(2,1)S(1)}, bf16[2,512,256]{2,1,0:T(8,128)(2,1)S(1)}, u32[]{:S(2)}, u32[]{:S(2)}) collective-permute-start(bf16[2,512,256]{2,1,0:T(8,128)(2,1)S(1)} %get-tuple-element.43), channel_id=1, source_target_pairs={{0,48},{1,49},{2,50},{3,51},{4,52},{5,53},{6,54},{7,55},{8,56},{9,... | collective-permute-start | bytes 1572872 | tf_op jit(solution)/shard_map/ppermute | solution.py:26
  175.5 21.8 %collective-permute-start.28 = (bf16[512,256]{1,0:T(8,128)(2,1)S(1)}, bf16[512,256]{1,0:T(8,128)(2,1)S(1)}, u32[]{:S(2)}, u32[]{:S(2)}) collective-permute-start(bf16[512,256]{1,0:T(8,128)(2,1)S(1)} %fusion.6), channel_id=1, source_target_pairs={{0,64},{1,65},{2,66},{3,67},{4,68},{5,69},{6,70},{7,71},{8,72},{9,... | collective-permute-start | bytes 786440 | tf_op jit(solution)/shard_map/ppermute | solution.py:26
  197.2 8.3 %collective-permute-start.35 = (bf16[512,256]{1,0:T(8,128)(2,1)S(1)}, bf16[512,256]{1,0:T(8,128)(2,1)S(1)}, u32[]{:S(2)}, u32[]{:S(2)}) collective-permute-start(bf16[512,256]{1,0:T(8,128)(2,1)S(1)} %fusion.7), channel_id=1, source_target_pairs={{0,64},{1,65},{2,66},{3,67},{4,68},{5,69},{6,70},{7,71},{8,72},{9,... | collective-permute-start | bytes 786440 | tf_op jit(solution)/shard_map/ppermute | solution.py:26
